TPU v7x, 32 devices: a whole 2x2x4 slice. The times are simulated.
32 devices in a mesh: pts: 16 (over z, y, core), grp: 2 (over x).
Axes of the slice: x: 2, y: 2, z: 4, core: 2. Of those that a mesh axis runs over, the one named last changes fastest.
Arguments:
- occ_orbitals: bfloat16 [4096, 1024], P('pts'), may hold values from -0.1875 to 0.1875
- virt_orbitals: bfloat16 [4096, 1024], P('pts'), may hold values from -0.1875 to 0.1875
- columns: bfloat16 [4096, 512], P('pts'), may hold values from -6 to 6
- occ_energies: float32 [1024], replicated, may hold values from -3 to -0.1
- vir_energies: float32 [1024], replicated, may hold values from 0.1 to 3
- tau_index: int32 [8], replicated, may hold values from 0 to 15, as said below
- quad_weights: float32 [8], replicated, may hold values from 0.05 to 0.5
- frequencies: float32 [2], replicated, may hold values from 0.2 to 2
- distance_kept: int32 [16], replicated, may hold values 0 or 1
Outputs:
- response: float32 [2, 512, 4096], P(None, 'grp', 'pts')
Inputs may be any that keep to these rules, and one draw needn't show every extreme that they name: `tau_index`: all entries differ; 0 and 15 are always among them.
All inputs are finite; a program needn't handle non-finite values.
Results may differ from a plain program's by a relative error of at most 0.0026.
Values may be sent and summed in bfloat16 or wider, within the bound.
A program may use at most 64 MiB of HBM per device.

v0:
```python
import functools
import math

import jax
import jax.numpy as jnp
from jax import lax
from jax.experimental import pallas as pl
from jax.experimental.pallas import tpu as pltpu
from jax.sharding import PartitionSpec as P

MESH = pl.DeviceIdType.MESH
NT = (((1,), (1,)), ((), ()))
F32, BF16 = jnp.float32, jnp.bfloat16
ROWS, CORES = 2, 2
DOWN, UP, ACROSS, BESIDE = range(4)
TIMES_AT_ONCE = 4


def kernel(
    cycle, groups,
    occ_ref, vir_ref, col_ref, occ_e_ref, vir_e_ref, tau_ref, weight_ref, freq_ref, kept_ref,
    out_ref,
    occ_s, vir_s, gathered, chi, total, turned, turned_sent, landed, cos_rows,
    send_sem, recv_sem, sum_send_sem, sum_recv_sem,
):
    me, grp = lax.axis_index("pts"), lax.axis_index("grp")
    layers = cycle // (ROWS * CORES)
    layer, row, core = me // (ROWS * CORES), (me // CORES) % ROWS, me % CORES
    points, n_occ = occ_ref.shape
    n_vir, n_col = vir_ref.shape[1], col_ref.shape[1]
    n_tau, n_freq = tau_ref.shape[0], freq_ref.shape[0]
    part = points // groups
    pair = CORES * part
    share = n_col // groups

    def index(a, b, c):
        return (a * ROWS + b) * CORES + c

    def move(slot, target, way):
        rows = pl.ds(pl.multiple_of(slot * part, part), part)
        return pltpu.make_async_remote_copy(
            src_ref=gathered.at[rows],
            dst_ref=gathered.at[rows],
            send_sem=send_sem.at[way, slot],
            recv_sem=recv_sem.at[slot],
            device_id={"pts": target},
            device_id_type=MESH,
        )

    below, above = index(layer - 1, row, core), index(layer + 1, row, core)
    across, beside = index(layer, 1 - row, core), index(layer, row, 1 - core)

    mine = pl.ds(pl.multiple_of(grp * part, part), part)
    own = pl.ds(pl.multiple_of(me * part, part), part)
    gathered[own, :n_occ] = occ_ref[mine]
    gathered[own, n_occ:n_occ + n_vir] = vir_ref[mine]
    gathered[own, n_occ + n_vir:] = col_ref[mine]

    barrier = pltpu.get_barrier_semaphore()

    def greet(**where):
        pl.semaphore_signal(barrier, inc=1, device_id=where, device_id_type=MESH)

    greet(pts=across)
    greet(pts=beside)
    for step in range(1, groups):
        greet(grp=lax.rem(grp + step, groups))

    @pl.when(layer > 0)
    def _():
        greet(pts=below)

    @pl.when(layer < layers - 1)
    def _():
        greet(pts=above)

    ends = (layer == 0).astype(jnp.int32) + (layer == layers - 1).astype(jnp.int32)
    pl.semaphore_wait(barrier, groups + 3 - ends)

    @pl.when(layer > 0)
    def _():
        move(me, below, DOWN).start()

    @pl.when(layer < layers - 1)
    def _():
        move(me, above, UP).start()

    move(me, across, ACROSS).start()
    move(me, beside, BESIDE).start()

    total[...] = jnp.zeros_like(total)

    def scale(k, _):
        index_row = jnp.full((1, n_occ), tau_ref[k].astype(F32), F32)
        time = 0.05 * jnp.exp(index_row * jnp.float32(math.log(1.5)))
        rows = pl.ds(pl.multiple_of(k * points, points), points)
        decay = jnp.exp(occ_e_ref[...].reshape(1, n_occ) * time)
        occ_s[rows] = (occ_ref[...].astype(F32) * decay).astype(BF16)
        index_row = jnp.full((1, n_vir), tau_ref[k].astype(F32), F32)
        time = 0.05 * jnp.exp(index_row * jnp.float32(math.log(1.5)))
        decay = jnp.exp(-vir_e_ref[...].reshape(1, n_vir) * time)
        vir_s[rows] = (vir_ref[...].astype(F32) * decay).astype(BF16)
        for w in range(n_freq):
            cos_rows[w, k] = -weight_ref[k] * jnp.cos(freq_ref[w] * time[:, :pair])
        return 0

    lax.fori_loop(0, n_tau, scale, 0)

    def compute(a, b):
        slot = index(a, b, 0)
        rows = pl.ds(pl.multiple_of(slot * part, pair), pair)
        block_tau = TIMES_AT_ONCE

        def some_times(i, _):
            at = pl.ds(pl.multiple_of(i * block_tau * points, block_tau * points), block_tau * points)
            green_occ = lax.dot_general(
                occ_s[at], gathered[rows, :n_occ], NT, preferred_element_type=F32
            )
            green_vir = lax.dot_general(
                vir_s[at], gathered[rows, n_occ:n_occ + n_vir], NT, preferred_element_type=F32
            )
            product = green_occ * green_vir
            for w in range(n_freq):
                added = 0.0
                for j in range(block_tau):
                    added += cos_rows[w, i * block_tau + j] * product[j * points:(j + 1) * points]

                @pl.when(i == 0)
                def _():
                    chi[w] = added

                @pl.when(i > 0)
                def _():
                    chi[w] += added
            return 0

        lax.fori_loop(0, n_tau // block_tau, some_times, 0)
        lane = lax.broadcasted_iota(jnp.int32, (1, pair), 1)
        kept = jnp.where(
            lane < part,
            kept_ref[lax.rem(slot - me + cycle, cycle)].astype(F32),
            kept_ref[lax.rem(slot + 1 - me + cycle, cycle)].astype(F32),
        )
        for w in range(n_freq):
            total[w] += jnp.dot(
                (chi[w] * kept).astype(BF16),
                gathered[rows, n_occ + n_vir:],
                preferred_element_type=F32,
            )

    def inside(a):
        return jnp.logical_and(a >= 0, a < layers)

    def same_row_arrives(t):
        for way in (-1, 1):
            @pl.when(inside(layer + way * t))
            def _():
                slot = index(layer + way * t, row, core)
                move(slot, me, DOWN).wait_recv()
                onward = layer - way

                @pl.when(inside(onward))
                def _():
                    move(slot, index(onward, row, core), DOWN if way > 0 else UP).start()

                move(slot, across, ACROSS).start()
                move(slot, beside, BESIDE).start()

    def other_row_arrives(t, ways):
        for way in ways:
            @pl.when(inside(layer + way * t))
            def _():
                slot = index(layer + way * t, 1 - row, core)
                move(slot, me, DOWN).wait_recv()
                move(slot, beside, BESIDE).start()

    def work(t, b, ways):
        for way in ways:
            @pl.when(inside(layer + way * t))
            def _():
                move(index(layer + way * t, b, 1 - core), me, DOWN).wait_recv()
                compute(layer + way * t, b)

    work(0, row, (1,))

    def round_(t, _):
        same_row_arrives(t)

        @pl.when(t == 1)
        def _():
            other_row_arrives(0, (1,))

        @pl.when(t > 1)
        def _():
            other_row_arrives(t - 1, (-1, 1))

        def one(n, _):
            other = n // 2
            gap = t - other
            place = layer + gap * (2 * (n % 2) - 1)
            fresh = jnp.logical_or(gap > 0, n % 2 == 1)

            @pl.when(jnp.logical_and(inside(place), fresh))
            def _():
                b = row + other * (1 - 2 * row)
                move(index(place, b, 1 - core), me, DOWN).wait_recv()
                compute(place, b)
            return 0

        lax.fori_loop(0, 4, one, 0)
        return 0

    lax.fori_loop(1, layers, round_, 0)
    other_row_arrives(layers - 1, (-1, 1))

    def last(n, _):
        place = layer + (layers - 1) * (2 * n - 1)

        @pl.when(inside(place))
        def _():
            move(index(place, 1 - row, 1 - core), me, DOWN).wait_recv()
            compute(place, 1 - row)
        return 0

    lax.fori_loop(0, 2, last, 0)

    for w in range(n_freq):
        flipped = total[w].T
        turned[w] = flipped
        turned_sent[w] = flipped.astype(BF16)
    sums = []
    for step in range(1, groups):
        to = lax.rem(grp + step, groups)
        sums.append(
            pltpu.make_async_remote_copy(
                src_ref=turned_sent.at[:, pl.ds(pl.multiple_of(to * share, share), share)],
                dst_ref=landed.at[step - 1],
                send_sem=sum_send_sem.at[step - 1],
                recv_sem=sum_recv_sem.at[step - 1],
                device_id={"grp": to},
                device_id_type=MESH,
            )
        )
        sums[-1].start()

    def left(slot, _):
        a, b, c = slot // (ROWS * CORES), (slot // CORES) % ROWS, slot % CORES
        mine_core = c == core
        same = jnp.logical_and(mine_core, b == row)

        @pl.when(jnp.logical_and(same, jnp.logical_and(a >= layer, layer > 0)))
        def _():
            move(slot, below, DOWN).wait_send()

        @pl.when(jnp.logical_and(same, jnp.logical_and(a <= layer, layer < layers - 1)))
        def _():
            move(slot, above, UP).wait_send()

        @pl.when(same)
        def _():
            move(slot, across, ACROSS).wait_send()

        @pl.when(mine_core)
        def _():
            move(slot, beside, BESIDE).wait_send()
        return 0

    lax.fori_loop(0, cycle, left, 0)
    for copy in sums:
        copy.wait()
    answer = turned[:, pl.ds(pl.multiple_of(grp * share, share), share)]
    for step in range(groups - 1):
        answer = answer + landed[step].astype(F32)
    out_ref[...] = answer


def per_device(occ, vir, col, occ_e, vir_e, tau, weights, frequencies, kept):
    cycle, groups = lax.axis_size("pts"), lax.axis_size("grp")
    points, n_occ = occ.shape
    n_vir, n_col = vir.shape[1], col.shape[1]
    n_tau, n_freq = tau.shape[0], frequencies.shape[0]
    part, share = points // groups, n_col // groups
    vmem = pl.BlockSpec(memory_space=pltpu.VMEM)
    smem = pl.BlockSpec(memory_space=pltpu.SMEM)
    return pl.pallas_call(
        functools.partial(kernel, cycle, groups),
        out_shape=jax.ShapeDtypeStruct((n_freq, share, points), F32),
        in_specs=[vmem] * 5 + [smem] * 4,
        out_specs=vmem,
        scratch_shapes=[
            pltpu.VMEM((n_tau * points, n_occ), BF16),
            pltpu.VMEM((n_tau * points, n_vir), BF16),
            pltpu.VMEM((cycle * part, n_occ + n_vir + n_col), BF16),
            pltpu.VMEM((n_freq, points, CORES * part), F32),
            pltpu.VMEM((n_freq, points, n_col), F32),
            pltpu.VMEM((n_freq, n_col, points), F32),
            pltpu.VMEM((n_freq, n_col, points), BF16),
            pltpu.VMEM((groups - 1, n_freq, share, points), BF16),
            pltpu.VMEM((n_freq, n_tau, 1, CORES * part), F32),
            pltpu.SemaphoreType.DMA((4, cycle)),
            pltpu.SemaphoreType.DMA((cycle,)),
            pltpu.SemaphoreType.DMA((groups - 1,)),
            pltpu.SemaphoreType.DMA((groups - 1,)),
        ],
        compiler_params=pltpu.CompilerParams(
            collective_id=0, has_side_effects=True, vmem_limit_bytes=56 * 1024 * 1024
        ),
    )(occ, vir, col, occ_e, vir_e, tau, weights, frequencies, kept)


def solution(mesh):
    placed = (P("pts", None), P("pts", None), P("pts", None), P(), P(), P(), P(), P(), P())
    return jax.shard_map(
        per_device, mesh=mesh, in_specs=placed, out_specs=P(None, "grp", "pts"), check_vma=False
    )
```

profile of v0, /device:TPU:1, one launch (start us, length us, event | category | flops | bytes accessed | tf_op | source)
XLA Modules:
  0.0 80.5 jit_solution(3196795968241728540)
XLA Ops:
  0.0 78.6 %shard_map.91 = f32[2,256,256]{2,1,0:T(8,128)} custom-call(bf16[256,1024]{1,0:T(8,128)(2,1)} %occ_ref.1, bf16[256,1024]{1,0:T(8,128)(2,1)} %vir_ref.1, bf16[256,512]{1,0:T(8,128)(2,1)} %col_ref.1, f32[1024]{0:T(1024)} %occ_e_ref.1, f32[1024]{0:T(1024)} %vir_e_ref.1, s32[8]{0:T(128)} %tau_ref.1, f32[8]{0:T(128)} %weight_ref.1, f32[2]{0:T(128)} %freq_ref.1, ...), custom_call_target="tpu_custom_call" | custom-call | tf_op jit(solution)/shard_map/pallas_call | solution.py:285
  78.6 1.9 %copy.11 = f32[2,256,256]{2,1,0:T(8,128)} copy(f32[2,256,256]{2,1,0:T(8,128)} %shard_map.91) | data formatting | bytes 1048576
where the time goes:
time: 80.7 us; the launch traced here: 80.5 us
  Pallas kernels  78.6 us (97%)
  local copies, waits for them, and re-layouts  1.87 us (2%)
    pallas_call x1, Pallas kernels, per_device(): pl.pallas_call(functools.partial(kernel, cycle, groups), out_shape=jax.Sh...  78.6 us
    unnamed x1, local copies, waits for them, and re-layouts  1.87 us

commit v1 on v0

v1 whole, which is shorter than its diff:
```python
import functools
import math

import jax
import jax.numpy as jnp
from jax import lax
from jax.experimental import pallas as pl
from jax.experimental.pallas import tpu as pltpu
from jax.sharding import PartitionSpec as P

MESH = pl.DeviceIdType.MESH
NT = (((1,), (1,)), ((), ()))
F32, BF16 = jnp.float32, jnp.bfloat16
ROWS, CORES = 2, 2
DOWN, UP, ACROSS, BESIDE = range(4)
PIECES = 2


def kernel(
    cycle, groups,
    occ_ref, vir_ref, col_ref, occ_e_ref, vir_e_ref, tau_ref, weight_ref, freq_ref, kept_ref,
    out_ref,
    occ_s, vir_s, gathered, green_occ, total, turned, turned_sent, landed, cos_rows,
    send_sem, recv_sem, sum_send_sem, sum_recv_sem,
):
    me, grp = lax.axis_index("pts"), lax.axis_index("grp")
    layers = cycle // (ROWS * CORES)
    layer, row, core = me // (ROWS * CORES), (me // CORES) % ROWS, me % CORES
    points, n_occ = occ_ref.shape
    n_vir, n_col = vir_ref.shape[1], col_ref.shape[1]
    n_tau, n_freq = tau_ref.shape[0], freq_ref.shape[0]
    part = points // groups
    pair = CORES * part
    share = n_col // groups

    def index(a, b, c):
        return (a * ROWS + b) * CORES + c

    piece = part // PIECES

    def move(slot, h, target, way):
        rows = pl.ds(pl.multiple_of(slot * part + h * piece, piece), piece)
        return pltpu.make_async_remote_copy(
            src_ref=gathered.at[rows],
            dst_ref=gathered.at[rows],
            send_sem=send_sem.at[way, slot, h],
            recv_sem=recv_sem.at[slot, h],
            device_id={"pts": target},
            device_id_type=MESH,
        )

    def along_layers(a, h):
        near = jnp.logical_or(
            jnp.logical_and(layer == 1, a == 0),
            jnp.logical_and(layer == layers - 2, a == layers - 1),
        )
        far = jnp.logical_or(
            jnp.logical_and(layer == 0, a == layers - 1),
            jnp.logical_and(layer == layers - 1, a == 0),
        )
        return jnp.logical_or(near, jnp.logical_and(far, h == PIECES - 1))

    def passes_up(a, h):
        near = jnp.logical_and(layer == 0, a == 0)
        far = jnp.logical_and(jnp.logical_and(layer == layers - 2, a == 0), h == PIECES - 1)
        return jnp.logical_and(layer < layers - 1, jnp.logical_or(near, far))

    def passes_down(a, h):
        near = jnp.logical_and(layer == layers - 1, a == layers - 1)
        far = jnp.logical_and(jnp.logical_and(layer == 1, a == layers - 1), h == PIECES - 1)
        return jnp.logical_and(layer > 0, jnp.logical_or(near, far))

    below, above = index(layer - 1, row, core), index(layer + 1, row, core)
    across, beside = index(layer, 1 - row, core), index(layer, row, 1 - core)

    mine = pl.ds(pl.multiple_of(grp * part, part), part)
    own = pl.ds(pl.multiple_of(me * part, part), part)
    gathered[own, :n_occ] = occ_ref[mine]
    gathered[own, n_occ:n_occ + n_vir] = vir_ref[mine]
    gathered[own, n_occ + n_vir:] = col_ref[mine]

    barrier = pltpu.get_barrier_semaphore()

    def greet(**where):
        pl.semaphore_signal(barrier, inc=1, device_id=where, device_id_type=MESH)

    greet(pts=across)
    greet(pts=beside)
    for step in range(1, groups):
        greet(grp=lax.rem(grp + step, groups))

    @pl.when(layer > 0)
    def _():
        greet(pts=below)

    @pl.when(layer < layers - 1)
    def _():
        greet(pts=above)

    ends = (layer == 0).astype(jnp.int32) + (layer == layers - 1).astype(jnp.int32)
    pl.semaphore_wait(barrier, groups + 3 - ends)

    for h in range(PIECES):
        @pl.when(layer > 0)
        def _():
            move(me, h, below, DOWN).start()

        @pl.when(layer < layers - 1)
        def _():
            move(me, h, above, UP).start()

        move(me, h, across, ACROSS).start()
        move(me, h, beside, BESIDE).start()

    total[...] = jnp.zeros_like(total)

    def scale(k, _):
        index_row = jnp.full((1, n_occ), tau_ref[k].astype(F32), F32)
        time = 0.05 * jnp.exp(index_row * jnp.float32(math.log(1.5)))
        rows = pl.ds(pl.multiple_of(k * points, points), points)
        decay = jnp.exp(occ_e_ref[...].reshape(1, n_occ) * time)
        occ_s[rows] = (occ_ref[...].astype(F32) * decay).astype(BF16)
        index_row = jnp.full((1, n_vir), tau_ref[k].astype(F32), F32)
        time = 0.05 * jnp.exp(index_row * jnp.float32(math.log(1.5)))
        decay = jnp.exp(-vir_e_ref[...].reshape(1, n_vir) * time)
        vir_s[rows] = (vir_ref[...].astype(F32) * decay).astype(BF16)
        for w in range(n_freq):
            cos_rows[w, k] = -weight_ref[k] * jnp.cos(freq_ref[w] * time[:, :pair])
        return 0

    lax.fori_loop(0, n_tau, scale, 0)

    def compute(a, b):
        slot = index(a, b, 0)
        rows = pl.ds(pl.multiple_of(slot * part, pair), pair)
        green_occ[...] = lax.dot_general(
            occ_s[...], gathered[rows, :n_occ], NT, preferred_element_type=F32
        )
        green_vir = lax.dot_general(
            vir_s[...], gathered[rows, n_occ:n_occ + n_vir], NT, preferred_element_type=F32
        )
        product = green_occ[...] * green_vir
        chi = []
        for w in range(n_freq):
            chi.append(
                sum(cos_rows[w, k] * product[k * points:(k + 1) * points] for k in range(n_tau))
            )
        lane = lax.broadcasted_iota(jnp.int32, (1, pair), 1)
        kept = jnp.where(
            lane < part,
            kept_ref[lax.rem(slot - me + cycle, cycle)].astype(F32),
            kept_ref[lax.rem(slot + 1 - me + cycle, cycle)].astype(F32),
        )
        for w in range(n_freq):
            masked = chi[w] * kept
            high = masked.astype(BF16)
            low = (masked - high.astype(F32)).astype(BF16)
            cols = gathered[rows, n_occ + n_vir:]
            total[w] += jnp.dot(high, cols, preferred_element_type=F32) + jnp.dot(
                low, cols, preferred_element_type=F32
            )

    def inside(a):
        return jnp.logical_and(a >= 0, a < layers)

    def same_row_arrives(t, h):
        for way in (-1, 1):
            @pl.when(inside(layer + way * t))
            def _():
                a = layer + way * t
                slot = index(a, row, core)
                move(slot, h, me, DOWN).wait_recv()
                onward = layer - way

                @pl.when(inside(onward))
                def _():
                    move(slot, h, index(onward, row, core), DOWN if way > 0 else UP).start()

                @pl.when(jnp.logical_not(along_layers(a, h)))
                def _():
                    move(slot, h, across, ACROSS).start()

                move(slot, h, beside, BESIDE).start()

    def other_row_arrives(t, h):
        for way in (-1, 1):
            @pl.when(jnp.logical_and(inside(layer + way * t), jnp.logical_or(t > 0, way > 0)))
            def _():
                a = layer + way * t
                slot = index(a, 1 - row, core)
                move(slot, h, me, DOWN).wait_recv()

                @pl.when(passes_up(a, h))
                def _():
                    move(slot, h, above, UP).start()

                @pl.when(passes_down(a, h))
                def _():
                    move(slot, h, below, DOWN).start()

                move(slot, h, beside, BESIDE).start()

    def work(a, b):
        for h in range(PIECES):
            move(index(a, b, 1 - core), h, me, DOWN).wait_recv()
        compute(a, b)

    def round_(t, _):
        def arrive(h, _):
            same_row_arrives(t, h)

            @pl.when(t > 0)
            def _():
                other_row_arrives(t - 1, h)
            return 0

        @pl.when(t > 0)
        def _():
            lax.fori_loop(0, PIECES, arrive, 0)

        def one(n, _):
            other = n // 2
            gap = t - other
            place = layer + gap * (2 * (n % 2) - 1)
            fresh = jnp.logical_or(gap > 0, jnp.logical_and(gap == 0, n % 2 == 1))

            @pl.when(jnp.logical_and(inside(place), fresh))
            def _():
                work(place, row + other * (1 - 2 * row))
            return 0

        lax.fori_loop(0, 4, one, 0)
        return 0

    lax.fori_loop(0, layers + 1, round_, 0)

    for w in range(n_freq):
        flipped = total[w].T
        turned[w] = flipped
        turned_sent[w] = flipped.astype(BF16)
    sums = []
    for step in range(1, groups):
        to = lax.rem(grp + step, groups)
        sums.append(
            pltpu.make_async_remote_copy(
                src_ref=turned_sent.at[:, pl.ds(pl.multiple_of(to * share, share), share)],
                dst_ref=landed.at[step - 1],
                send_sem=sum_send_sem.at[step - 1],
                recv_sem=sum_recv_sem.at[step - 1],
                device_id={"grp": to},
                device_id_type=MESH,
            )
        )
        sums[-1].start()

    def left(n, _):
        slot, h = n // PIECES, n % PIECES
        a, b, c = slot // (ROWS * CORES), (slot // CORES) % ROWS, slot % CORES

        @pl.when(c == core)
        def _():
            same, other = b == row, b != row
            down = jnp.logical_and(same, jnp.logical_and(a >= layer, layer > 0))
            up = jnp.logical_and(same, jnp.logical_and(a <= layer, layer < layers - 1))

            @pl.when(jnp.logical_or(down, jnp.logical_and(other, passes_down(a, h))))
            def _():
                move(slot, h, below, DOWN).wait_send()

            @pl.when(jnp.logical_or(up, jnp.logical_and(other, passes_up(a, h))))
            def _():
                move(slot, h, above, UP).wait_send()

            @pl.when(jnp.logical_and(same, jnp.logical_not(along_layers(a, h))))
            def _():
                move(slot, h, across, ACROSS).wait_send()

            move(slot, h, beside, BESIDE).wait_send()
        return 0

    lax.fori_loop(0, cycle * PIECES, left, 0)
    for copy in sums:
        copy.wait()
    answer = turned[:, pl.ds(pl.multiple_of(grp * share, share), share)]
    for step in range(groups - 1):
        answer = answer + landed[step].astype(F32)
    out_ref[...] = answer


def per_device(occ, vir, col, occ_e, vir_e, tau, weights, frequencies, kept):
    cycle, groups = lax.axis_size("pts"), lax.axis_size("grp")
    points, n_occ = occ.shape
    n_vir, n_col = vir.shape[1], col.shape[1]
    n_tau, n_freq = tau.shape[0], frequencies.shape[0]
    part, share = points // groups, n_col // groups
    vmem = pl.BlockSpec(memory_space=pltpu.VMEM)
    smem = pl.BlockSpec(memory_space=pltpu.SMEM)
    return pl.pallas_call(
        functools.partial(kernel, cycle, groups),
        out_shape=jax.ShapeDtypeStruct((n_freq, share, points), F32),
        in_specs=[vmem] * 5 + [smem] * 4,
        out_specs=vmem,
        scratch_shapes=[
            pltpu.VMEM((n_tau * points, n_occ), BF16),
            pltpu.VMEM((n_tau * points, n_vir), BF16),
            pltpu.VMEM((cycle * part, n_occ + n_vir + n_col), BF16),
            pltpu.VMEM((n_tau * points, CORES * part), F32),
            pltpu.VMEM((n_freq, points, n_col), F32),
            pltpu.VMEM((n_freq, n_col, points), F32),
            pltpu.VMEM((n_freq, n_col, points), BF16),
            pltpu.VMEM((groups - 1, n_freq, share, points), BF16),
            pltpu.VMEM((n_freq, n_tau, 1, CORES * part), F32),
            pltpu.SemaphoreType.DMA((4, cycle, PIECES)),
            pltpu.SemaphoreType.DMA((cycle, PIECES)),
            pltpu.SemaphoreType.DMA((groups - 1,)),
            pltpu.SemaphoreType.DMA((groups - 1,)),
        ],
        compiler_params=pltpu.CompilerParams(
            collective_id=0, has_side_effects=True, vmem_limit_bytes=56 * 1024 * 1024
        ),
    )(occ, vir, col, occ_e, vir_e, tau, weights, frequencies, kept)


def solution(mesh):
    placed = (P("pts", None), P("pts", None), P("pts", None), P(), P(), P(), P(), P(), P())
    return jax.shard_map(
        per_device, mesh=mesh, in_specs=placed, out_specs=P(None, "grp", "pts"), check_vma=False
    )
```

time: 80.7 us -> 73.8 us (0.914)
  Pallas kernels: 78.6 us -> 71.4 us
    pallas_call x1, Pallas kernels: 78.6 us -> 71.4 us  [per_device(): pl.pallas_call(functools.partial(kernel, cycle, groups), out_shape=jax.Sh...]
where the time goes in v1:
time: 73.8 us; the launch traced here: 73.3 us
  Pallas kernels  71.4 us (97%)
  local copies, waits for them, and re-layouts  1.87 us (3%)
    pallas_call x1, Pallas kernels, per_device(): pl.pallas_call(functools.partial(kernel, cycle, groups), out_shape=jax.Sh...  71.4 us
    unnamed x1, local copies, waits for them, and re-layouts  1.87 us

profile of v1, /device:TPU:1, one launch (start us, length us, event | category | flops | bytes accessed | tf_op | source)
XLA Modules:
  0.0 73.3 jit_solution(7011461547952447422)
XLA Ops:
  0.0 71.4 %shard_map.91 = f32[2,256,256]{2,1,0:T(8,128)} custom-call(bf16[256,1024]{1,0:T(8,128)(2,1)} %occ_ref.1, bf16[256,1024]{1,0:T(8,128)(2,1)} %vir_ref.1, bf16[256,512]{1,0:T(8,128)(2,1)} %col_ref.1, f32[1024]{0:T(1024)} %occ_e_ref.1, f32[1024]{0:T(1024)} %vir_e_ref.1, s32[8]{0:T(128)} %tau_ref.1, f32[8]{0:T(128)} %weight_ref.1, f32[2]{0:T(128)} %freq_ref.1, ...), custom_call_target="tpu_custom_call" | custom-call | tf_op jit(solution)/shard_map/pallas_call | solution.py:298
  71.5 1.9 %copy.11 = f32[2,256,256]{2,1,0:T(8,128)} copy(f32[2,256,256]{2,1,0:T(8,128)} %shard_map.91) | data formatting | bytes 1048576
